TPU v7x, 32 devices: a whole 2x2x4 slice. The times are simulated.
32 devices in a mesh: grp: 2 (over y), fsdp: 8 (over z, x), seq: 2 (over core).
Axes of the slice: x: 2, y: 2, z: 4, core: 2. Of those that a mesh axis runs over, the one named last changes fastest.
Arguments:
- image_tokens: bfloat16 [16, 512, 3072], P(('grp', 'fsdp'), 'seq'), parts along dimension 0, may hold values from -6 to 6
- adjoint: bfloat16 [16, 512, 3072], P(('grp', 'fsdp'), 'seq'), parts along dimension 0, may hold values from -24 to 24
- attn_keys: bfloat16 [16, 768, 1536], P(('grp', 'fsdp'), 'seq'), parts along dimension 0, may hold values from -2.5 to 2.5
- attn_values: bfloat16 [16, 768, 1536], P(('grp', 'fsdp'), 'seq'), parts along dimension 0, may hold values from -6 to 6
- w_query: bfloat16 [3072, 1536], P('fsdp', 'seq'), may hold values from -0.109375 to 0.109375
- w_out: bfloat16 [1536, 3072], P('seq', 'fsdp'), may hold values from -0.15625 to 0.15625
- q_gain: float32 [128], replicated, may hold values from 1 to 2.5
- mod_table: float32 [28, 3, 3072], replicated, may hold values from -4 to 4
- timesteps: int32 [16], P(('grp', 'fsdp')), parts along dimension 0, may hold values from 0 to 27
- text_counts: int32 [16], P(('grp', 'fsdp')), parts along dimension 0, may hold values from 1 to 256
Outputs:
- branch_cotangent: float32 [16, 512, 3072], P(('grp', 'fsdp'), 'seq'), parts along dimension 0
There are 2 independent parts, one for each index of `grp`. A program takes and returns all parts, laid end to end along the dimension named above; an argument that names none is the same for every part. Nothing has to cross between parts.
Inputs may be any that keep to these rules, and one draw needn't show every extreme that they name: Of a prompt's 256 text keys, the first text_counts of them are real and the rest are padding.
All inputs are finite; a program needn't handle non-finite values.
Results may differ from a plain program's by a relative error of at most 0.0092.
Values may be sent and summed in bfloat16 or wider, within the bound.
A program may use at most 128 MiB of HBM per device.

v0:
```python
import jax
import jax.numpy as jnp
from jax import lax
from jax.sharding import PartitionSpec as P

HD = 128
SWAP = ((0, 1), (1, 0))


def contract_last(left, right):
    return lax.dot_general(
        left, right, (((1,), (1,)), ((), ())), preferred_element_type=jnp.float32
    )


def swap(piece):
    return lax.ppermute(piece, "seq", SWAP)


def local(
    image_tokens,
    adjoint,
    attn_keys,
    attn_values,
    w_query,
    w_out,
    q_gain,
    mod_table,
    timesteps,
    text_counts,
):
    me = lax.axis_index("seq")
    half = w_query.shape[1]
    heads = half // HD
    factor = HD ** (-0.5)
    w_q = lax.all_gather(w_query, "fsdp", axis=0, tiled=True)
    w_o = lax.all_gather(w_out.T, "fsdp", axis=0, tiled=True)
    modulation = lax.dynamic_index_in_dim(mod_table, timesteps[0], 0, keepdims=False)
    shift_row, scale_row, gate_row = (modulation[0], modulation[1], modulation[2])
    tokens = image_tokens[0].astype(jnp.float32)
    mean = jnp.mean(tokens, axis=-1, keepdims=True)
    centred = tokens - mean
    inv = lax.rsqrt(jnp.mean(centred * centred, axis=-1, keepdims=True) + 1e-06)
    normed = (centred * inv * (1.0 + scale_row) + shift_row).astype(jnp.bfloat16)
    d_branch = (gate_row * adjoint[0].astype(jnp.float32)).astype(jnp.bfloat16)

    def halves(rows):
        own = lax.dynamic_slice_in_dim(rows, me * half, half, 1)
        other = lax.dynamic_slice_in_dim(rows, (1 - me) * half, half, 1)
        return jnp.concatenate([own, swap(other)], axis=0)

    keys, values = (halves(attn_keys[0]), halves(attn_values[0]))
    key_rows = attn_keys.shape[1]
    txt = keys.shape[0] // 3
    spots = jnp.arange(key_rows, dtype=jnp.int32)
    positions = jnp.concatenate([me * key_rows + spots, (1 - me) * key_rows + spots])
    usable = (positions >= txt) | (positions < text_counts[0])
    normed_all = jnp.concatenate([normed, swap(normed)], axis=0)
    d_branch_all = jnp.concatenate([d_branch, swap(d_branch)], axis=0)
    query = jnp.dot(normed_all, w_q, preferred_element_type=jnp.float32)
    d_attn = jnp.dot(d_branch_all, w_o, preferred_element_type=jnp.float32).astype(jnp.bfloat16)
    parts = []
    for head in range(heads):
        cols = slice(head * HD, (head + 1) * HD)
        q_head, k_head, v_head = (query[:, cols], keys[:, cols], values[:, cols])
        root = lax.rsqrt(jnp.mean(q_head * q_head, axis=-1, keepdims=True) + 1e-06)
        unit = q_head * root
        q_normed = (unit * q_gain).astype(jnp.bfloat16)
        scores = contract_last(q_normed, k_head) * factor
        terms = jnp.where(usable[None, :], jnp.exp(scores), 0.0)
        probs = terms / jnp.sum(terms, axis=-1, keepdims=True)
        d_probs = contract_last(d_attn[:, cols], v_head)
        centre = jnp.sum(probs * d_probs, axis=-1, keepdims=True)
        d_scores = (probs * (d_probs - centre) * factor).astype(jnp.bfloat16)
        d_unit = jnp.dot(d_scores, k_head, preferred_element_type=jnp.float32) * q_gain
        d_query = root * (d_unit - unit * jnp.mean(d_unit * unit, axis=-1, keepdims=True))
        parts.append(d_query.astype(jnp.bfloat16))
    d_query = jnp.concatenate(parts, axis=1)
    count = tokens.shape[0]
    theirs = contract_last(d_query[count:], w_q).astype(jnp.bfloat16)
    mine = contract_last(d_query[:count], w_q)
    d_normed = mine + swap(theirs).astype(jnp.float32)
    d_hat = d_normed * (1.0 + scale_row)
    hat = centred * inv
    d_mean = jnp.mean(d_hat, axis=-1, keepdims=True)
    d_proj = jnp.mean(d_hat * hat, axis=-1, keepdims=True)
    return (inv * (d_hat - d_mean - hat * d_proj))[None]


def solution(mesh):
    in_specs = (
        P(("grp", "fsdp"), "seq", None),
        P(("grp", "fsdp"), "seq", None),
        P(("grp", "fsdp"), "seq", None),
        P(("grp", "fsdp"), "seq", None),
        P("fsdp", "seq"),
        P("seq", "fsdp"),
        P(),
        P(),
        P(("grp", "fsdp")),
        P(("grp", "fsdp")),
    )
    out_specs = P(("grp", "fsdp"), "seq", None)
    return jax.shard_map(local, mesh=mesh, in_specs=in_specs, out_specs=out_specs, check_vma=False)
```

profile of v0, /device:TPU:0, one launch (start us, length us, event | category | flops | bytes accessed | tf_op | source)
XLA Modules:
  0.0 214.6 jit_solution(10942834821170242803)
XLA Ops:
  8.7 1.7 convert_reduce_fusion
  12.0 1.9 fusion.7
  16.8 1.5 fusion.21
  19.5 72.7 %all-gather.3.cloned.1.call-done = bf16[3072,768]{1,0:T(8,128)(2,1)} async-done(((bf16[384,768]{1,0:T(8,128)(2,1)}), bf16[3072,768]{1,0:T(8,128)(2,1)}) %all-gather.3.cloned.1.call-update) | async-done | bytes 4718608 | tf_op jit(solution)/shard_map/all_gather | solution.py:36
  92.2 5.9 %fusion.13 = f32[512,768]{1,0:T(8,128)S(1)} fusion(bf16[3072,768]{1,0:T(8,128)(2,1)} %all-gather.3.cloned.1.call-done, bf16[256,3072]{1,0:T(8,128)(2,1)} %collective-permute-done, bf16[256,3072]{1,0:T(8,128)(2,1)} %fusion.7), kind=kOutput, calls=%fused_computation.16 | convolution fusion | flops 2422210560 | bytes 9437184 | tf_op jit(solution)/shard_map/dot_general | solution.py:60
  98.7 2.2 %fusion.116 = (f32[512]{0:T(512)}, f32[512,768]{1,0:T(8,128)}) fusion(bf16[384,768]{1,0:T(8,128)(2,1)S(1)} %get-tuple-element.20, bf16[384,768]{1,0:T(8,128)(2,1)S(1)} %collective-permute-done.1, f32[512,768]{1,0:T(8,128)S(1)} %fusion.13, f32[512]{0:T(512)S(1)} %get-tuple-element.56, f32[128]{0:T(128)S(1)} %copy-done.23, pred[768]{0:T(1024)(128)(4,1)S(1)} %compare_or_fusion), kind=kOutput, calls=%fused_computation.213 | convolution fusion | flops 102432256 | bytes 3020288 | tf_op jit(solution)/shard_map/dot_general | solution.py:11
  101.0 2.2 %fusion.111 = (f32[512]{0:T(512)}, f32[512,768]{1,0:T(8,128)}) fusion(bf16[384,768]{1,0:T(8,128)(2,1)S(1)} %get-tuple-element.20, bf16[384,768]{1,0:T(8,128)(2,1)S(1)} %collective-permute-done.1, f32[512,768]{1,0:T(8,128)S(1)} %fusion.13, f32[128]{0:T(128)S(1)} %copy-done.23, f32[512]{0:T(512)S(1)} %get-tuple-element.57, pred[768]{0:T(1024)(128)(4,1)S(1)} %compare_or_fusion), kind=kOutput, calls=%fused_computation.208 | convolution fusion | flops 102432256 | bytes 3020288 | tf_op jit(solution)/shard_map/dot_general | solution.py:11
  103.2 2.3 %fusion.114 = (f32[512]{0:T(512)}, f32[512,768]{1,0:T(8,128)}) fusion(bf16[384,768]{1,0:T(8,128)(2,1)S(1)} %get-tuple-element.20, bf16[384,768]{1,0:T(8,128)(2,1)S(1)} %collective-permute-done.1, f32[512,768]{1,0:T(8,128)S(1)} %fusion.13, f32[512]{0:T(512)S(1)} %get-tuple-element.54, f32[128]{0:T(128)S(1)} %copy-done.23, pred[768]{0:T(1024)(128)(4,1)S(1)} %compare_or_fusion), kind=kOutput, calls=%fused_computation.211 | convolution fusion | flops 102432256 | bytes 3020288 | tf_op jit(solution)/shard_map/dot_general | solution.py:11
  105.5 2.2 %fusion.115 = (f32[512]{0:T(512)}, f32[512,768]{1,0:T(8,128)}) fusion(bf16[384,768]{1,0:T(8,128)(2,1)S(1)} %get-tuple-element.20, bf16[384,768]{1,0:T(8,128)(2,1)S(1)} %collective-permute-done.1, f32[512,768]{1,0:T(8,128)S(1)} %fusion.13, f32[512]{0:T(512)S(1)} %get-tuple-element.55, f32[128]{0:T(128)S(1)} %copy-done.23, pred[768]{0:T(1024)(128)(4,1)S(1)} %compare_or_fusion), kind=kOutput, calls=%fused_computation.212 | convolution fusion | flops 102432256 | bytes 3020288 | tf_op jit(solution)/shard_map/dot_general | solution.py:11
  107.7 2.2 %fusion.113 = (f32[512]{0:T(512)}, f32[512,768]{1,0:T(8,128)}) fusion(bf16[384,768]{1,0:T(8,128)(2,1)S(1)} %get-tuple-element.20, bf16[384,768]{1,0:T(8,128)(2,1)S(1)} %collective-permute-done.1, f32[512,768]{1,0:T(8,128)S(1)} %fusion.13, f32[512]{0:T(512)S(1)} %get-tuple-element.53, f32[128]{0:T(128)S(1)} %copy-done.23, pred[768]{0:T(1024)(128)(4,1)S(1)} %compare_or_fusion), kind=kOutput, calls=%fused_computation.210 | convolution fusion | flops 102432256 | bytes 3020288 | tf_op jit(solution)/shard_map/dot_general | solution.py:11
  109.9 2.2 %fusion.112 = (f32[512]{0:T(512)}, f32[512,768]{1,0:T(8,128)}) fusion(bf16[768,128]{1,0:T(8,128)(2,1)S(1)} %pad_maximum_fusion.2, f32[512,768]{1,0:T(8,128)S(1)} %fusion.13, f32[512]{0:T(512)S(1)} %get-tuple-element.52, f32[128]{0:T(128)S(1)} %copy-done.23, pred[768]{0:T(1024)(128)(4,1)S(1)} %compare_or_fusion), kind=kOutput, calls=%fused_computation.209 | convolution fusion | flops 102039040 | bytes 2037248 | tf_op jit(solution)/shard_map/dot_general | solution.py:11
  112.1 61.2 %all-gather.5.cloned.1.call-done = bf16[3072,768]{0,1:T(8,128)(2,1)} async-done(((bf16[384,768]{0,1:T(8,128)(2,1)}), bf16[3072,768]{0,1:T(8,128)(2,1)}) %all-gather.5.cloned.1.call-update) | async-done | bytes 4718608 | tf_op jit(solution)/shard_map/all_gather | solution.py:37
  173.4 6.0 %fusion.22 = bf16[512,768]{1,0:T(8,128)(2,1)S(1)} fusion(bf16[3072,768]{0,1:T(8,128)(2,1)} %all-gather.5.cloned.1.call-done, bf16[256,3072]{1,0:T(8,128)(2,1)} %collective-permute-done.2, bf16[256,3072]{1,0:T(8,128)(2,1)} %fusion.21), kind=kOutput, calls=%fused_computation.65 | convolution fusion | flops 2422603776 | bytes 8650752 | tf_op jit(solution)/shard_map/dot_general | solution.py:61
  179.5 1.4 multiply_reduce_fusion.4
  182.3 1.4 multiply_reduce_fusion.5
  185.1 1.4 multiply_reduce_fusion.2
  187.9 1.4 multiply_reduce_fusion.3
  190.6 1.5 multiply_reduce_fusion.1
  192.1 1.4 multiply_reduce_fusion
  195.0 1.2 multiply_reduce_fusion.6
  197.8 1.4 convolution_convert_fusion
  199.3 3.4 %collective-permute-done.4 = bf16[256,3072]{1,0:T(8,128)(2,1)S(1)} collective-permute-done((bf16[256,3072]{1,0:T(8,128)(2,1)S(1)}, bf16[256,3072]{1,0:T(8,128)(2,1)S(1)}, u32[]{:S(2)}, u32[]{:S(2)}) %collective-permute-start.4) | collective-permute-done | bytes 1572896 | tf_op jit(solution)/shard_map/ppermute | solution.py:17
  202.7 2.0 fusion.25
  204.7 3.0 %fusion.11 = f32[1,256,3072]{2,1,0:T(8,128)} fusion(bf16[1,256,3072]{2,1,0:T(8,128)(2,1)S(1)} %copy-done, f32[256]{0:T(256)S(1)} %broadcast_multiply_fusion.6, f32[256]{0:T(256)S(1)} %broadcast_multiply_fusion.7, f32[256]{0:T(256)S(1)} %copy-done.26, f32[256]{0:T(256)S(1)} %copy-done.22, f32[3072]{0:T(1024)S(1)} %bitcast.60, ...), kind=kLoop, calls=%fused_computation.14 | loop fusion | flops 7864320 | bytes 9453568 | tf_op jit(solution)/shard_map/broadcast_in_dim | solution.py:87
  (122 shorter events, 15.6 us)
Async XLA Ops:
  6.5 3.8 %copy-start = (bf16[1,256,3072]{2,1,0:T(8,128)(2,1)S(1)}, bf16[1,256,3072]{2,1,0:T(8,128)(2,1)}, u32[]{:S(2)}) copy-start(bf16[1,256,3072]{2,1,0:T(8,128)(2,1)} %param.10) | copy-start | bytes 4718596
  6.5 85.6 %all-gather.3.cloned.1.call-start = ((), (), s32[]{:S(2)}) async-start(), calls=%async_computation | async-start | bytes 5308416 | tf_op jit(solution)/shard_map/all_gather | solution.py:36
  7.3 166.1 %all-gather.5.cloned.1.call-start = ((), (), s32[]{:S(2)}) async-start(), calls=%async_computation.1 | async-start | bytes 5308416 | tf_op jit(solution)/shard_map/all_gather | solution.py:37
  10.4 3.6 %copy-start.21 = (f32[256]{0:T(256)}, f32[256]{0:T(256)S(1)}, u32[]{:S(2)}) copy-start(f32[256]{0:T(256)S(1)} %broadcast_multiply_fusion.8) | copy-start | bytes 3076
  10.9 3.0 %copy-start.25 = (f32[256]{0:T(256)}, f32[256]{0:T(256)S(1)}, u32[]{:S(2)}) copy-start(f32[256]{0:T(256)S(1)} %add_rsqrt_fusion.6) | copy-start | bytes 3076
  12.0 2.4 %copy-start.9 = (bf16[1,384,1536]{2,1,0:T(8,128)(2,1)S(1)}, bf16[1,384,1536]{2,1,0:T(8,128)(2,1)}, u32[]{:S(2)}) copy-start(bf16[1,384,1536]{2,1,0:T(8,128)(2,1)} %param.12) | copy-start | bytes 3538948
  13.9 5.5 %collective-permute-start = (bf16[256,3072]{1,0:T(8,128)(2,1)}, bf16[256,3072]{1,0:T(8,128)(2,1)}, u32[]{:S(2)}, u32[]{:S(2)}) collective-permute-start(bf16[256,3072]{1,0:T(8,128)(2,1)} %fusion.7), channel_id=1, source_target_pairs={{0,1},{1,0},{2,3},{3,2},{4,5},{5,4},{6,7},{7,6},{8,9},{9,8},{10,11... | collective-permute-start | bytes 4718600 | tf_op jit(solution)/shard_map/ppermute | solution.py:17
  15.3 4.2 %collective-permute-start.1 = (bf16[384,768]{1,0:T(8,128)(2,1)}, bf16[384,768]{1,0:T(8,128)(2,1)S(1)}, u32[]{:S(2)}, u32[]{:S(2)}) collective-permute-start(bf16[384,768]{1,0:T(8,128)(2,1)} %get-tuple-element.19), channel_id=1, source_target_pairs={{0,1},{1,0},{2,3},{3,2},{4,5},{5,4},{6,7},{7,6},{8,9},{9,8},{10,11... | collective-permute-start | bytes 1769480 | tf_op jit(solution)/shard_map/ppermute | solution.py:17
  16.8 162.7 %collective-permute-start.3 = (bf16[384,768]{1,0:T(8,128)(2,1)}, bf16[384,768]{1,0:T(8,128)(2,1)}, u32[]{:S(2)}, u32[]{:S(2)}) collective-permute-start(bf16[384,768]{1,0:T(8,128)(2,1)} %get-tuple-element.24), channel_id=1, source_target_pairs={{0,1},{1,0},{2,3},{3,2},{4,5},{5,4},{6,7},{7,6},{8,9},{9,8},{10,11... | collective-permute-start | bytes 1769480 | tf_op jit(solution)/shard_map/ppermute | solution.py:17
  18.3 93.9 %collective-permute-start.2 = (bf16[256,3072]{1,0:T(8,128)(2,1)}, bf16[256,3072]{1,0:T(8,128)(2,1)}, u32[]{:S(2)}, u32[]{:S(2)}) collective-permute-start(bf16[256,3072]{1,0:T(8,128)(2,1)} %fusion.21), channel_id=1, source_target_pairs={{0,1},{1,0},{2,3},{3,2},{4,5},{5,4},{6,7},{7,6},{8,9},{9,8},{10,11... | collective-permute-start | bytes 4718600 | tf_op jit(solution)/shard_map/ppermute | solution.py:17
  98.1 11.8 %copy-start.1 = (f32[512,768]{1,0:T(8,128)}, f32[512,768]{1,0:T(8,128)S(1)}, u32[]{:S(2)}) copy-start(f32[512,768]{1,0:T(8,128)S(1)} %fusion.13) | copy-start | bytes 4718596
  98.6 9.1 %copy-start.11 = (f32[512]{0:T(512)}, f32[512]{0:T(512)S(1)}, u32[]{:S(2)}) copy-start(f32[512]{0:T(512)S(1)} %get-tuple-element.53) | copy-start | bytes 6148
  98.6 11.3 %copy-start.27 = (f32[512]{0:T(512)}, f32[512]{0:T(512)S(1)}, u32[]{:S(2)}) copy-start(f32[512]{0:T(512)S(1)} %get-tuple-element.52) | copy-start | bytes 6148
  98.6 2.3 %copy-start.15 = (f32[512]{0:T(512)}, f32[512]{0:T(512)S(1)}, u32[]{:S(2)}) copy-start(f32[512]{0:T(512)S(1)} %get-tuple-element.56) | copy-start | bytes 6148
  98.6 4.6 %copy-start.17 = (f32[512]{0:T(512)}, f32[512]{0:T(512)S(1)}, u32[]{:S(2)}) copy-start(f32[512]{0:T(512)S(1)} %get-tuple-element.57) | copy-start | bytes 6148
  101.0 4.5 %copy-start.13 = (f32[512]{0:T(512)}, f32[512]{0:T(512)S(1)}, u32[]{:S(2)}) copy-start(f32[512]{0:T(512)S(1)} %get-tuple-element.54) | copy-start | bytes 6148
  101.0 4.5 %copy-start.19 = (f32[512]{0:T(512)}, f32[512]{0:T(512)S(1)}, u32[]{:S(2)}) copy-start(f32[512]{0:T(512)S(1)} %get-tuple-element.55) | copy-start | bytes 6148
  112.1 67.3 %copy-start.32 = (f32[512]{0:T(512)S(1)}, f32[512]{0:T(512)}, u32[]{:S(2)}) copy-start(f32[512]{0:T(512)} %get-tuple-element.46) | copy-start | bytes 6148
  173.4 6.1 %copy-start.7 = (f32[512,768]{1,0:T(8,128)S(1)}, f32[512,768]{1,0:T(8,128)}, u32[]{:S(2)}) copy-start(f32[512,768]{1,0:T(8,128)} %get-tuple-element.47) | copy-start | bytes 4718596
  193.6 4.1 %slice-start = ((s8[4718592]{0:T(1024)(128)(4,1)}), s8[4194304]{0:T(1024)(128)(4,1)S(1)}, s32[]{:S(2)}) async-start(s8[4718592]{0:T(1024)(128)(4,1)} %bitcast.63), calls=%async_computation.2 | async-start | bytes 8388608
  195.0 2.8 %slice-start.1 = ((s8[4718592]{0:T(1024)(128)(4,1)}), s8[524288]{0:T(1024)(128)(4,1)S(1)}, s32[]{:S(2)}) async-start(s8[4718592]{0:T(1024)(128)(4,1)} %bitcast.63), calls=%async_computation.3 | async-start | bytes 1048576
  197.7 4.9 %copy-start.22 = (f32[256]{0:T(256)S(1)}, f32[256]{0:T(256)}, u32[]{:S(2)}) copy-start(f32[256]{0:T(256)} %copy-done.21) | copy-start | bytes 3076
  197.7 4.9 %copy-start.26 = (f32[256]{0:T(256)S(1)}, f32[256]{0:T(256)}, u32[]{:S(2)}) copy-start(f32[256]{0:T(256)} %copy-done.25) | copy-start | bytes 3076
  199.2 3.5 %collective-permute-start.4 = (bf16[256,3072]{1,0:T(8,128)(2,1)S(1)}, bf16[256,3072]{1,0:T(8,128)(2,1)S(1)}, u32[]{:S(2)}, u32[]{:S(2)}) collective-permute-start(bf16[256,3072]{1,0:T(8,128)(2,1)S(1)} %convolution_convert_fusion), channel_id=1, source_target_pairs={{0,1},{1,0},{2,3},{3,2},{4,5},{5,4},{6,7},{7,6},{8,9},{9,8},{10,11... | collective-permute-start | bytes 4718600 | tf_op jit(solution)/shard_map/ppermute | solution.py:17
  (21 other events, 29.2 us)
Sparse Core Ops, SparseCore 0:
  9.5 82.5 all-gather.2
  94.2 79.1 all-gather.4
where the time goes:
time: 215 us
  waiting for transfers between devices  139 us (65%)
  matrix products  40.9 us (19%)
  between operations  15.3 us (7%)
  other arithmetic  11.8 us (5%)
  local copies, waits for them, and re-layouts  6.78 us (3%)
    all_gather x1, waiting for transfers between devices, local(): w_q = lax.all_gather(w_query, 'fsdp', axis=0, tiled=True)  72.7 us
    all_gather x1, waiting for transfers between devices, local(): w_o = lax.all_gather(w_out.T, 'fsdp', axis=0, tiled=True)  61.2 us
    dot_general x14, matrix products, contract_last(): lax.dot_general(left, right, (((1,), (1,)), ((), ())), preferred_element_...  25.1 us
    dot_general x1, matrix products, local(): jnp.dot(d_branch_all, w_o, preferred_element_type=jnp.float32)  6.04 us
    dot_general x1, matrix products, local(): query = jnp.dot(normed_all, w_q, preferred_element_type=jnp.float32)  5.89 us
    unnamed x76, local copies, waits for them, and re-layouts  5.01 us
  transfers between devices with their start and end apart: 7, of which 3 were waited for; matrix products, arithmetic and copies ran while one was open for 16% of the time, Pallas kernels for 0%

commit v1 on v0

--- a/solution.py
+++ b/solution.py
@@ -33,7 +33,22 @@
     half = w_query.shape[1]
     heads = half // HD
     factor = HD ** (-0.5)
-    w_q = lax.all_gather(w_query, "fsdp", axis=0, tiled=True)
+    ways, here, step = (lax.axis_size("fsdp"), lax.axis_index("fsdp"), w_query.shape[0])
+    shape = [n * ways if d == 0 else n for d, n in enumerate(w_query.shape)]
+    w_q = lax.dynamic_update_slice_in_dim(
+        jnp.zeros(shape, w_query.dtype), w_query, here * step, axis=0
+    )
+    going_up = going_down = w_query
+    for far in range(1, ways // 2 + 1):
+        going_up = lax.ppermute(going_up, "fsdp", [(d, (d + 1) % ways) for d in range(ways)])
+        w_q = lax.dynamic_update_slice_in_dim(w_q, going_up, (here - far) % ways * step, axis=0)
+        if 2 * far < ways:
+            going_down = lax.ppermute(
+                going_down, "fsdp", [(d, (d - 1) % ways) for d in range(ways)]
+            )
+            w_q = lax.dynamic_update_slice_in_dim(
+                w_q, going_down, (here + far) % ways * step, axis=0
+            )
     w_o = lax.all_gather(w_out.T, "fsdp", axis=0, tiled=True)
     modulation = lax.dynamic_index_in_dim(mod_table, timesteps[0], 0, keepdims=False)
     shift_row, scale_row, gate_row = (modulation[0], modulation[1], modulation[2])

time: 215 us -> 196 us (0.912)
  waiting for transfers between devices: 139 us -> 97 us
  starting transfers between devices: 1.13 us -> 19.5 us
  local copies, waits for them, and re-layouts: 6.78 us -> 12.8 us
    ppermute x0 -> x7, waiting for transfers between devices: none -> 92.9 us  [the longest x4 80.6 us: local(): lax.ppermute(going_up, 'fsdp', [(d, (d + 1) % ways) for d in range(ways)])]
    all_gather x1 -> x0, waiting for transfers between devices: 72.7 us -> none  [local(): w_q = lax.all_gather(w_query, 'fsdp', axis=0, tiled=True)]
    all_gather x1, waiting for transfers between devices: 61.2 us -> 0.01 us  [local(): w_o = lax.all_gather(w_out.T, 'fsdp', axis=0, tiled=True)]
    ppermute x0 -> x7, starting transfers between devices: none -> 18.8 us  [the longest x3 10.2 us: local(): lax.ppermute(going_down, 'fsdp', [(d, (d - 1) % ways) for d in range(ways)])]
    dynamic_update_slice x0 -> x8, local copies, waits for them, and re-layouts: none -> 3.68 us  [the longest x4 2.45 us: local(): lax.dynamic_update_slice_in_dim(w_q, going_up, (here - far) % ways * step...]
    unnamed x76 -> x78, local copies, waits for them, and re-layouts: 5.01 us -> 5.58 us
  transfers between devices with their start and end apart: 7 -> 13, of which waited for: 3 -> 6; matrix products, arithmetic and copies ran while one was open for 16% -> 20% of each run, Pallas kernels for 0% -> 0%
where the time goes in v1:
time: 196 us
  waiting for transfers between devices  97 us (49%)
  matrix products  41.1 us (21%)
  starting transfers between devices  19.5 us (10%)
  between operations  15.3 us (8%)
  local copies, waits for them, and re-layouts  12.8 us (7%)
  other arithmetic  10.1 us (5%)
    ppermute x4, waiting for transfers between devices, local(): lax.ppermute(going_up, 'fsdp', [(d, (d + 1) % ways) for d in range(ways)])  80.6 us
    dot_general x14, matrix products, contract_last(): lax.dot_general(left, right, (((1,), (1,)), ((), ())), preferred_element_...  25.3 us
    ppermute x3, waiting for transfers between devices, local(): lax.ppermute(going_down, 'fsdp', [(d, (d - 1) % ways) for d in range(ways)])  12.3 us
    ppermute x3, starting transfers between devices, local(): lax.ppermute(going_down, 'fsdp', [(d, (d - 1) % ways) for d in range(ways)])  10.2 us
    ppermute x4, starting transfers between devices, local(): lax.ppermute(going_up, 'fsdp', [(d, (d + 1) % ways) for d in range(ways)])  8.59 us
    dot_general x1, matrix products, local(): query = jnp.dot(normed_all, w_q, preferred_element_type=jnp.float32)  6.18 us
    dot_general x1, matrix products, local(): jnp.dot(d_branch_all, w_o, preferred_element_type=jnp.float32)  6.07 us
    unnamed x78, local copies, waits for them, and re-layouts  5.58 us
  transfers between devices with their start and end apart: 13, of which 6 were waited for; matrix products, arithmetic and copies ran while one was open for 20% of the time, Pallas kernels for 0%

profile of v1, /device:TPU:0, one launch (start us, length us, event | category | flops | bytes accessed | tf_op | source)
XLA Modules:
  0.0 195.8 jit_solution(11499667579504784950)
XLA Ops:
  7.3 3.0 %collective-permute-start.1 = (bf16[384,768]{1,0:T(8,128)(2,1)}, bf16[384,768]{1,0:T(8,128)(2,1)}, u32[]{:S(2)}, u32[]{:S(2)}) collective-permute-start(bf16[384,768]{1,0:T(8,128)(2,1)} %param.14), channel_id=1, source_target_pairs={{0,2},{2,4},{4,6},{6,8},{8,10},{10,12},{12,14},{14,0},{1,3},{3,5},... | collective-permute-start | bytes 1769480 | tf_op jit(solution)/shard_map/ppermute | solution.py:43
  10.2 3.1 %collective-permute-start.2 = (bf16[384,768]{1,0:T(8,128)(2,1)}, bf16[384,768]{1,0:T(8,128)(2,1)S(1)}, u32[]{:S(2)}, u32[]{:S(2)}) collective-permute-start(bf16[384,768]{1,0:T(8,128)(2,1)} %param.14), channel_id=1, source_target_pairs={{0,14},{2,0},{4,2},{6,4},{8,6},{10,8},{12,10},{14,12},{1,15},{3,1}... | collective-permute-start | bytes 1769480 | tf_op jit(solution)/shard_map/ppermute | solution.py:46
  13.4 2.1 %dynamic-slice_bitcast_fusion.2 = (bf16[384,768]{1,0:T(8,128)(2,1)}, bf16[384,768]{1,0:T(8,128)(2,1)S(1)}) fusion(bf16[1,384,1536]{2,1,0:T(8,128)(2,1)} %param.12, s32[]{:T(128)S(6)} %select_n.103, s32[]{:T(128)S(6)} %select_n.102), kind=kLoop, calls=%fused_computation.93 | loop fusion | bytes 2359304 | tf_op jit(solution)/shard_map/dynamic_slice | solution.py:64
  18.1 1.9 fusion.8
  21.7 20.4 %collective-permute-done.1 = bf16[384,768]{1,0:T(8,128)(2,1)} collective-permute-done((bf16[384,768]{1,0:T(8,128)(2,1)}, bf16[384,768]{1,0:T(8,128)(2,1)}, u32[]{:S(2)}, u32[]{:S(2)}) %collective-permute-start.1) | collective-permute-done | bytes 589856 | tf_op jit(solution)/shard_map/ppermute | solution.py:43
  42.1 2.5 %collective-permute-start.3 = (bf16[384,768]{1,0:T(8,128)(2,1)}, bf16[384,768]{1,0:T(8,128)(2,1)}, u32[]{:S(2)}, u32[]{:S(2)}) collective-permute-start(bf16[384,768]{1,0:T(8,128)(2,1)} %collective-permute-done.1), channel_id=1, source_target_pairs={{0,2},{2,4},{4,6},{6,8},{8,10},{10,12},{12,14},{14,0},{1,3},{3,5},... | collective-permute-start | bytes 1769480 | tf_op jit(solution)/shard_map/ppermute | solution.py:43
  44.6 3.0 %collective-permute-start.4 = (bf16[384,768]{1,0:T(8,128)(2,1)S(1)}, bf16[384,768]{1,0:T(8,128)(2,1)}, u32[]{:S(2)}, u32[]{:S(2)}) collective-permute-start(bf16[384,768]{1,0:T(8,128)(2,1)S(1)} %collective-permute-done.2), channel_id=1, source_target_pairs={{0,14},{2,0},{4,2},{6,4},{8,6},{10,8},{12,10},{14,12},{1,15},{3,1}... | collective-permute-start | bytes 1769480 | tf_op jit(solution)/shard_map/ppermute | solution.py:46
  49.8 21.2 %collective-permute-done.3 = bf16[384,768]{1,0:T(8,128)(2,1)} collective-permute-done((bf16[384,768]{1,0:T(8,128)(2,1)}, bf16[384,768]{1,0:T(8,128)(2,1)}, u32[]{:S(2)}, u32[]{:S(2)}) %collective-permute-start.3) | collective-permute-done | bytes 589856 | tf_op jit(solution)/shard_map/ppermute | solution.py:43
  74.2 4.0 %collective-permute-start.6 = (bf16[384,768]{1,0:T(8,128)(2,1)}, bf16[384,768]{1,0:T(8,128)(2,1)S(1)}, u32[]{:S(2)}, u32[]{:S(2)}) collective-permute-start(bf16[384,768]{1,0:T(8,128)(2,1)} %collective-permute-done.4), channel_id=1, source_target_pairs={{0,14},{2,0},{4,2},{6,4},{8,6},{10,8},{12,10},{14,12},{1,15},{3,1}... | collective-permute-start | bytes 1769480 | tf_op jit(solution)/shard_map/ppermute | solution.py:46
  78.3 31.9 %collective-permute-done.5 = bf16[384,768]{1,0:T(8,128)(2,1)S(1)} collective-permute-done((bf16[384,768]{1,0:T(8,128)(2,1)}, bf16[384,768]{1,0:T(8,128)(2,1)S(1)}, u32[]{:S(2)}, u32[]{:S(2)}) %collective-permute-start.5) | collective-permute-done | bytes 589856 | tf_op jit(solution)/shard_map/ppermute | solution.py:43
  110.2 2.4 %collective-permute-start.7 = (bf16[384,768]{1,0:T(8,128)(2,1)S(1)}, bf16[384,768]{1,0:T(8,128)(2,1)S(1)}, u32[]{:S(2)}, u32[]{:S(2)}) collective-permute-start(bf16[384,768]{1,0:T(8,128)(2,1)S(1)} %collective-permute-done.5), channel_id=1, source_target_pairs={{0,2},{2,4},{4,6},{6,8},{8,10},{10,12},{12,14},{14,0},{1,3},{3,5},... | collective-permute-start | bytes 1769480 | tf_op jit(solution)/shard_map/ppermute | solution.py:43
  114.9 12.3 %collective-permute-done.6 = bf16[384,768]{1,0:T(8,128)(2,1)S(1)} collective-permute-done((bf16[384,768]{1,0:T(8,128)(2,1)}, bf16[384,768]{1,0:T(8,128)(2,1)S(1)}, u32[]{:S(2)}, u32[]{:S(2)}) %collective-permute-start.6) | collective-permute-done | bytes 589856 | tf_op jit(solution)/shard_map/ppermute | solution.py:46
  127.2 7.1 %collective-permute-done.7 = bf16[384,768]{1,0:T(8,128)(2,1)S(1)} collective-permute-done((bf16[384,768]{1,0:T(8,128)(2,1)S(1)}, bf16[384,768]{1,0:T(8,128)(2,1)S(1)}, u32[]{:S(2)}, u32[]{:S(2)}) %collective-permute-start.7) | collective-permute-done | bytes 589856 | tf_op jit(solution)/shard_map/ppermute | solution.py:43
  134.4 6.2 %fusion.14 = f32[512,768]{1,0:T(8,128)S(1)} fusion(bf16[3072,768]{1,0:T(8,128)(2,1)S(1)} %constant_dynamic-update-slice_fusion, bf16[256,3072]{1,0:T(8,128)(2,1)} %collective-permute-done, bf16[256,3072]{1,0:T(8,128)(2,1)} %fusion.8), kind=kOutput, calls=%fused_computation.18 | convolution fusion | flops 2422210560 | bytes 9437184 | tf_op jit(solution)/shard_map/dot_general | solution.py:75
  141.2 2.2 %fusion.111 = (f32[512]{0:T(512)}, f32[512,768]{1,0:T(8,128)}) fusion(bf16[384,768]{1,0:T(8,128)(2,1)S(1)} %get-tuple-element.20, bf16[384,768]{1,0:T(8,128)(2,1)S(1)} %collective-permute-done.8, f32[512,768]{1,0:T(8,128)S(1)} %fusion.14, f32[128]{0:T(128)S(1)} %copy-done.24, f32[512]{0:T(512)S(1)} %get-tuple-element.57, pred[768]{0:T(1024)(128)(4,1)S(1)} %compare_or_fusion), kind=kOutput, calls=%fused_computation.216 | convolution fusion | flops 102432256 | bytes 3020288 | tf_op jit(solution)/shard_map/dot_general | solution.py:11
  143.5 2.2 %fusion.113 = (f32[512]{0:T(512)}, f32[512,768]{1,0:T(8,128)}) fusion(bf16[384,768]{1,0:T(8,128)(2,1)S(1)} %get-tuple-element.20, bf16[384,768]{1,0:T(8,128)(2,1)S(1)} %collective-permute-done.8, f32[512,768]{1,0:T(8,128)S(1)} %fusion.14, f32[512]{0:T(512)S(1)} %get-tuple-element.53, f32[128]{0:T(128)S(1)} %copy-done.24, pred[768]{0:T(1024)(128)(4,1)S(1)} %compare_or_fusion), kind=kOutput, calls=%fused_computation.218 | convolution fusion | flops 102432256 | bytes 3020288 | tf_op jit(solution)/shard_map/dot_general | solution.py:11
  145.7 2.2 %fusion.114 = (f32[512]{0:T(512)}, f32[512,768]{1,0:T(8,128)}) fusion(bf16[384,768]{1,0:T(8,128)(2,1)S(1)} %get-tuple-element.20, bf16[384,768]{1,0:T(8,128)(2,1)S(1)} %collective-permute-done.8, f32[512,768]{1,0:T(8,128)S(1)} %fusion.14, f32[512]{0:T(512)S(1)} %get-tuple-element.54, f32[128]{0:T(128)S(1)} %copy-done.24, pred[768]{0:T(1024)(128)(4,1)S(1)} %compare_or_fusion), kind=kOutput, calls=%fused_computation.219 | convolution fusion | flops 102432256 | bytes 3020288 | tf_op jit(solution)/shard_map/dot_general | solution.py:11
  148.0 2.3 %fusion.115 = (f32[512]{0:T(512)}, f32[512,768]{1,0:T(8,128)}) fusion(bf16[384,768]{1,0:T(8,128)(2,1)S(1)} %get-tuple-element.20, bf16[384,768]{1,0:T(8,128)(2,1)S(1)} %collective-permute-done.8, f32[512,768]{1,0:T(8,128)S(1)} %fusion.14, f32[512]{0:T(512)S(1)} %get-tuple-element.55, f32[128]{0:T(128)S(1)} %copy-done.24, pred[768]{0:T(1024)(128)(4,1)S(1)} %compare_or_fusion), kind=kOutput, calls=%fused_computation.220 | convolution fusion | flops 102432256 | bytes 3020288 | tf_op jit(solution)/shard_map/dot_general | solution.py:11
  150.2 2.2 %fusion.116 = (f32[512]{0:T(512)}, f32[512,768]{1,0:T(8,128)}) fusion(bf16[384,768]{1,0:T(8,128)(2,1)S(1)} %get-tuple-element.20, bf16[384,768]{1,0:T(8,128)(2,1)S(1)} %collective-permute-done.8, f32[512,768]{1,0:T(8,128)S(1)} %fusion.14, f32[512]{0:T(512)S(1)} %get-tuple-element.56, f32[128]{0:T(128)S(1)} %copy-done.24, pred[768]{0:T(1024)(128)(4,1)S(1)} %compare_or_fusion), kind=kOutput, calls=%fused_computation.221 | convolution fusion | flops 102432256 | bytes 3020288 | tf_op jit(solution)/shard_map/dot_general | solution.py:11
  152.5 2.2 %fusion.112 = (f32[512]{0:T(512)}, f32[512,768]{1,0:T(8,128)}) fusion(bf16[768,128]{1,0:T(8,128)(2,1)S(1)} %pad_maximum_fusion.2, f32[512,768]{1,0:T(8,128)S(1)} %fusion.14, f32[512]{0:T(512)S(1)} %get-tuple-element.52, f32[128]{0:T(128)S(1)} %copy-done.24, pred[768]{0:T(1024)(128)(4,1)S(1)} %compare_or_fusion), kind=kOutput, calls=%fused_computation.217 | convolution fusion | flops 102039040 | bytes 2037248 | tf_op jit(solution)/shard_map/dot_general | solution.py:11
  154.7 6.1 %fusion.23 = bf16[512,768]{1,0:T(8,128)(2,1)S(1)} fusion(bf16[3072,768]{0,1:T(8,128)(2,1)} %all-gather.2.cloned.1.call-done, bf16[256,3072]{1,0:T(8,128)(2,1)} %collective-permute-done.9, bf16[256,3072]{1,0:T(8,128)(2,1)} %fusion.22), kind=kOutput, calls=%fused_computation.66 | convolution fusion | flops 2422603776 | bytes 8650752 | tf_op jit(solution)/shard_map/dot_general | solution.py:76
  180.9 3.4 %collective-permute-done.11 = bf16[256,3072]{1,0:T(8,128)(2,1)S(1)} collective-permute-done((bf16[256,3072]{1,0:T(8,128)(2,1)S(1)}, bf16[256,3072]{1,0:T(8,128)(2,1)S(1)}, u32[]{:S(2)}, u32[]{:S(2)}) %collective-permute-start.11) | collective-permute-done | bytes 1572896 | tf_op jit(solution)/shard_map/ppermute | solution.py:17
  184.3 1.9 fusion.110
  186.2 2.8 %fusion.12 = f32[1,256,3072]{2,1,0:T(8,128)} fusion(bf16[1,256,3072]{2,1,0:T(8,128)(2,1)S(1)} %copy-done, f32[256,3072]{1,0:T(8,128)S(1)} %get-tuple-element.51, f32[256]{0:T(256)S(1)} %broadcast_multiply_fusion.6, f32[256]{0:T(256)S(1)} %broadcast_multiply_fusion.7, f32[256]{0:T(256)S(1)} %copy-done.27, f32[256]{0:T(256)S(1)} %copy-done.23), kind=kLoop, calls=%fused_computation.16 | loop fusion | flops 5505024 | bytes 7868416 | tf_op jit(solution)/shard_map/broadcast_in_dim | solution.py:102
  (144 shorter events, 31.8 us)
Async XLA Ops:
  6.5 9.6 %copy-start = (bf16[1,256,3072]{2,1,0:T(8,128)(2,1)S(1)}, bf16[1,256,3072]{2,1,0:T(8,128)(2,1)}, u32[]{:S(2)}) copy-start(bf16[1,256,3072]{2,1,0:T(8,128)(2,1)} %param.10) | copy-start | bytes 4718596
  6.5 148.2 %all-gather.2.cloned.1.call-start = ((), (), s32[]{:S(2)}) async-start(), calls=%async_computation | async-start | bytes 5308416 | tf_op jit(solution)/shard_map/all_gather | solution.py:52
  7.3 34.9 %collective-permute-start.1 = (bf16[384,768]{1,0:T(8,128)(2,1)}, bf16[384,768]{1,0:T(8,128)(2,1)}, u32[]{:S(2)}, u32[]{:S(2)}) collective-permute-start(bf16[384,768]{1,0:T(8,128)(2,1)} %param.14), channel_id=1, source_target_pairs={{0,2},{2,4},{4,6},{6,8},{8,10},{10,12},{12,14},{14,0},{1,3},{3,5},... | collective-permute-start | bytes 1769480 | tf_op jit(solution)/shard_map/ppermute | solution.py:43
  10.2 34.3 %collective-permute-start.2 = (bf16[384,768]{1,0:T(8,128)(2,1)}, bf16[384,768]{1,0:T(8,128)(2,1)S(1)}, u32[]{:S(2)}, u32[]{:S(2)}) collective-permute-start(bf16[384,768]{1,0:T(8,128)(2,1)} %param.14), channel_id=1, source_target_pairs={{0,14},{2,0},{4,2},{6,4},{8,6},{10,8},{12,10},{14,12},{1,15},{3,1}... | collective-permute-start | bytes 1769480 | tf_op jit(solution)/shard_map/ppermute | solution.py:46
  15.5 62.8 %collective-permute-start.8 = (bf16[384,768]{1,0:T(8,128)(2,1)}, bf16[384,768]{1,0:T(8,128)(2,1)S(1)}, u32[]{:S(2)}, u32[]{:S(2)}) collective-permute-start(bf16[384,768]{1,0:T(8,128)(2,1)} %get-tuple-element.19), channel_id=1, source_target_pairs={{0,1},{1,0},{2,3},{3,2},{4,5},{5,4},{6,7},{7,6},{8,9},{9,8},{10,11... | collective-permute-start | bytes 1769480 | tf_op jit(solution)/shard_map/ppermute | solution.py:17
  20.0 27.6 %copy-start.4 = (bf16[1,256,3072]{2,1,0:T(8,128)(2,1)S(1)}, bf16[1,256,3072]{2,1,0:T(8,128)(2,1)}, u32[]{:S(2)}) copy-start(bf16[1,256,3072]{2,1,0:T(8,128)(2,1)} %param.11) | copy-start | bytes 4718596
  20.0 114.3 %collective-permute-start = (bf16[256,3072]{1,0:T(8,128)(2,1)}, bf16[256,3072]{1,0:T(8,128)(2,1)}, u32[]{:S(2)}, u32[]{:S(2)}) collective-permute-start(bf16[256,3072]{1,0:T(8,128)(2,1)} %fusion.8), channel_id=1, source_target_pairs={{0,1},{1,0},{2,3},{3,2},{4,5},{5,4},{6,7},{7,6},{8,9},{9,8},{10,11... | collective-permute-start | bytes 4718600 | tf_op jit(solution)/shard_map/ppermute | solution.py:17
  21.6 139.2 %collective-permute-start.10 = (bf16[384,768]{1,0:T(8,128)(2,1)}, bf16[384,768]{1,0:T(8,128)(2,1)}, u32[]{:S(2)}, u32[]{:S(2)}) collective-permute-start(bf16[384,768]{1,0:T(8,128)(2,1)} %get-tuple-element.24), channel_id=1, source_target_pairs={{0,1},{1,0},{2,3},{3,2},{4,5},{5,4},{6,7},{7,6},{8,9},{9,8},{10,11... | collective-permute-start | bytes 1769480 | tf_op jit(solution)/shard_map/ppermute | solution.py:17
  42.1 28.9 %collective-permute-start.3 = (bf16[384,768]{1,0:T(8,128)(2,1)}, bf16[384,768]{1,0:T(8,128)(2,1)}, u32[]{:S(2)}, u32[]{:S(2)}) collective-permute-start(bf16[384,768]{1,0:T(8,128)(2,1)} %collective-permute-done.1), channel_id=1, source_target_pairs={{0,2},{2,4},{4,6},{6,8},{8,10},{10,12},{12,14},{14,0},{1,3},{3,5},... | collective-permute-start | bytes 1769480 | tf_op jit(solution)/shard_map/ppermute | solution.py:43
  44.6 29.6 %collective-permute-start.4 = (bf16[384,768]{1,0:T(8,128)(2,1)S(1)}, bf16[384,768]{1,0:T(8,128)(2,1)}, u32[]{:S(2)}, u32[]{:S(2)}) collective-permute-start(bf16[384,768]{1,0:T(8,128)(2,1)S(1)} %collective-permute-done.2), channel_id=1, source_target_pairs={{0,14},{2,0},{4,2},{6,4},{8,6},{10,8},{12,10},{14,12},{1,15},{3,1}... | collective-permute-start | bytes 1769480 | tf_op jit(solution)/shard_map/ppermute | solution.py:46
  71.0 39.2 %collective-permute-start.5 = (bf16[384,768]{1,0:T(8,128)(2,1)}, bf16[384,768]{1,0:T(8,128)(2,1)S(1)}, u32[]{:S(2)}, u32[]{:S(2)}) collective-permute-start(bf16[384,768]{1,0:T(8,128)(2,1)} %collective-permute-done.3), channel_id=1, source_target_pairs={{0,2},{2,4},{4,6},{6,8},{8,10},{10,12},{12,14},{14,0},{1,3},{3,5},... | collective-permute-start | bytes 1769480 | tf_op jit(solution)/shard_map/ppermute | solution.py:43
  72.9 5.4 %copy-start.5 = (bf16[256,3072]{1,0:T(8,128)(2,1)S(1)}, bf16[256,3072]{1,0:T(8,128)(2,1)}, u32[]{:S(2)}) copy-start(bf16[256,3072]{1,0:T(8,128)(2,1)} %fusion.22) | copy-start | bytes 4718596
  74.2 53.0 %collective-permute-start.6 = (bf16[384,768]{1,0:T(8,128)(2,1)}, bf16[384,768]{1,0:T(8,128)(2,1)S(1)}, u32[]{:S(2)}, u32[]{:S(2)}) collective-permute-start(bf16[384,768]{1,0:T(8,128)(2,1)} %collective-permute-done.4), channel_id=1, source_target_pairs={{0,14},{2,0},{4,2},{6,4},{8,6},{10,8},{12,10},{14,12},{1,15},{3,1}... | collective-permute-start | bytes 1769480 | tf_op jit(solution)/shard_map/ppermute | solution.py:46
  78.3 76.5 %collective-permute-start.9 = (bf16[256,3072]{1,0:T(8,128)(2,1)S(1)}, bf16[256,3072]{1,0:T(8,128)(2,1)}, u32[]{:S(2)}, u32[]{:S(2)}) collective-permute-start(bf16[256,3072]{1,0:T(8,128)(2,1)S(1)} %copy-done.5), channel_id=1, source_target_pairs={{0,1},{1,0},{2,3},{3,2},{4,5},{5,4},{6,7},{7,6},{8,9},{9,8},{10,11... | collective-permute-start | bytes 4718600 | tf_op jit(solution)/shard_map/ppermute | solution.py:17
  110.2 24.1 %collective-permute-start.7 = (bf16[384,768]{1,0:T(8,128)(2,1)S(1)}, bf16[384,768]{1,0:T(8,128)(2,1)S(1)}, u32[]{:S(2)}, u32[]{:S(2)}) collective-permute-start(bf16[384,768]{1,0:T(8,128)(2,1)S(1)} %collective-permute-done.5), channel_id=1, source_target_pairs={{0,2},{2,4},{4,6},{6,8},{8,10},{10,12},{12,14},{14,0},{1,3},{3,5},... | collective-permute-start | bytes 1769480 | tf_op jit(solution)/shard_map/ppermute | solution.py:43
  134.3 6.2 %copy-start.3 = (bf16[3072,768]{1,0:T(8,128)(2,1)}, bf16[3072,768]{1,0:T(8,128)(2,1)S(1)}, u32[]{:S(2)}) copy-start(bf16[3072,768]{1,0:T(8,128)(2,1)S(1)} %constant_dynamic-update-slice_fusion) | copy-start | bytes 14155780
  140.6 11.9 %copy-start.1 = (f32[512,768]{1,0:T(8,128)}, f32[512,768]{1,0:T(8,128)S(1)}, u32[]{:S(2)}) copy-start(f32[512,768]{1,0:T(8,128)S(1)} %fusion.14) | copy-start | bytes 4718596
  141.1 9.1 %copy-start.14 = (f32[512]{0:T(512)}, f32[512]{0:T(512)S(1)}, u32[]{:S(2)}) copy-start(f32[512]{0:T(512)S(1)} %get-tuple-element.56) | copy-start | bytes 6148
  141.1 11.3 %copy-start.28 = (f32[512]{0:T(512)}, f32[512]{0:T(512)S(1)}, u32[]{:S(2)}) copy-start(f32[512]{0:T(512)S(1)} %get-tuple-element.52) | copy-start | bytes 6148
  154.7 6.1 %copy-start.13 = (bf16[384,768]{1,0:T(8,128)(2,1)S(1)}, bf16[384,768]{1,0:T(8,128)(2,1)}, u32[]{:S(2)}) copy-start(bf16[384,768]{1,0:T(8,128)(2,1)} %get-tuple-element.25) | copy-start | bytes 1769476
  154.7 6.1 %copy-start.10 = (f32[512,768]{1,0:T(8,128)S(1)}, f32[512,768]{1,0:T(8,128)}, u32[]{:S(2)}) copy-start(f32[512,768]{1,0:T(8,128)} %get-tuple-element.27) | copy-start | bytes 4718596
  179.4 4.9 %copy-start.23 = (f32[256]{0:T(256)S(1)}, f32[256]{0:T(256)}, u32[]{:S(2)}) copy-start(f32[256]{0:T(256)} %copy-done.22) | copy-start | bytes 3076
  179.4 4.9 %copy-start.27 = (f32[256]{0:T(256)S(1)}, f32[256]{0:T(256)}, u32[]{:S(2)}) copy-start(f32[256]{0:T(256)} %copy-done.26) | copy-start | bytes 3076
  180.8 3.5 %collective-permute-start.11 = (bf16[256,3072]{1,0:T(8,128)(2,1)S(1)}, bf16[256,3072]{1,0:T(8,128)(2,1)S(1)}, u32[]{:S(2)}, u32[]{:S(2)}) collective-permute-start(bf16[256,3072]{1,0:T(8,128)(2,1)S(1)} %convolution_convert_fusion), channel_id=1, source_target_pairs={{0,1},{1,0},{2,3},{3,2},{4,5},{5,4},{6,7},{7,6},{8,9},{9,8},{10,11... | collective-permute-start | bytes 4718600 | tf_op jit(solution)/shard_map/ppermute | solution.py:17
  (28 other events, 57.0 us)
Sparse Core Ops, SparseCore 0:
  9.4 142.0 all-gather.1
